TPU v7x, 32 devices: a whole 2x2x4 slice. The times are simulated.
32 devices in a mesh: space: 4 (over y, core), angle: 8 (over z, x).
Axes of the slice: x: 2, y: 2, z: 4, core: 2. Of those that a mesh axis runs over, the one named last changes fastest.
Arguments:
- image: float32 [16384, 128], P(('space', 'angle')), may hold values from 0 to 1
- tiles: bfloat16 [4, 768, 128, 128], P('space', 'angle'), may hold values from -0.109375 to 0.109375
- tile_slot: int32 [4, 768], P('space', 'angle'), may hold values from 0 to 7, as said below
- tile_block: int32 [4, 768], P('space', 'angle'), may hold values from 0 to 31
- slot_ray: int32 [4, 64], P('space', 'angle'), may hold values from 0 to 15, as said below
- sinogram: bfloat16 [8, 16, 128, 128], P('angle', 'space'), may hold values from -4 to 4
- weights: bfloat16 [8, 16, 128, 128], P('angle', 'space'), may hold values from 0.29882812 to 3
Outputs:
- volume: float32 [16384, 128], P(('space', 'angle'))
- residual: bfloat16 [8, 16, 128, 128], P('angle', 'space')
Inputs may be any that keep to these rules, and one draw needn't show every extreme that they name: `tile_slot`: every slot of a device is fed by at least one of its tiles. `slot_ray`: the 8 entries of one device are distinct; of the ray blocks k * 4 to (k + 1) * 4 - 1 of its angle group, one device lists at most 2, and in every angle group some k is listed 2 times by every device of the group.
All inputs are finite; a program needn't handle non-finite values.
Results may differ from a plain program's by a relative error of at most 0.025.
Values may be sent and summed in bfloat16 or wider, within the bound.
A program may use at most 64 MiB of HBM per device.

v0:
```python
import math

import jax
import jax.numpy as jnp
from jax import lax
from jax.sharding import PartitionSpec as P

CAP = 2
ITERS = 2


def shards(image, tiles, tile_slot, tile_block, slot_ray, sinogram, weights):
    n_space = lax.axis_size("space")
    n_angle = lax.axis_size("angle")
    tile_mats = tiles[0]
    slot_ids = tile_slot[0]
    block_ids = tile_block[0]
    ray_ids = slot_ray[0]
    own_count = sinogram.shape[1]
    tile_edge = tile_mats.shape[1]
    slices = image.shape[1]
    share_rows = image.shape[0]
    block_count = share_rows * n_angle // tile_edge
    slot_count = ray_ids.shape[0]
    step_size = 0.2 * math.sqrt(block_count / (n_angle * own_count))
    observed = sinogram[0].astype(jnp.float32)
    scales = weights[0].astype(jnp.float32)
    slot_hot = (slot_ids[:, None] == jnp.arange(slot_count, dtype=jnp.int32)[None, :]).astype(
        jnp.float32
    )
    block_hot = (block_ids[:, None] == jnp.arange(block_count, dtype=jnp.int32)[None, :]).astype(
        jnp.float32
    )
    owner_ids = ray_ids // own_count
    owner_hot = (owner_ids[:, None] == jnp.arange(n_space, dtype=jnp.int32)[None, :]).astype(
        jnp.int32
    )
    seat_rank = jnp.sum((jnp.cumsum(owner_hot, axis=0) - owner_hot) * owner_hot, axis=1)
    seat_index = owner_ids * CAP + seat_rank
    seat_table = seat_index[None, :] == jnp.arange(n_space * CAP, dtype=jnp.int32)[:, None]
    place_hot = seat_table.astype(jnp.bfloat16)
    send_ids = jnp.sum(seat_table.astype(jnp.int32) * (ray_ids % own_count + 1)[None, :], axis=1)
    got_ids = lax.all_to_all(
        send_ids.reshape(n_space, CAP), "space", split_axis=0, concat_axis=0, tiled=True
    ).reshape(-1)
    gather_hot = (got_ids[None, :] - 1 == jnp.arange(own_count, dtype=jnp.int32)[:, None]).astype(
        jnp.bfloat16
    )

    def ray_residual(partial_value):
        outgoing = jnp.einsum(
            "ps,sik->pik", place_hot, partial_value, preferred_element_type=jnp.float32
        ).astype(jnp.bfloat16)
        incoming = lax.all_to_all(
            outgoing.reshape(n_space, CAP, tile_edge, slices),
            "space",
            split_axis=0,
            concat_axis=0,
            tiled=True,
        )
        ray_sums = jnp.einsum(
            "op,pik->oik",
            gather_hot,
            incoming.reshape(n_space * CAP, tile_edge, slices),
            preferred_element_type=jnp.float32,
        )
        residual = (scales * (ray_sums - observed)).astype(jnp.bfloat16)
        returned = jnp.einsum(
            "op,oik->pik", gather_hot, residual, preferred_element_type=jnp.float32
        ).astype(jnp.bfloat16)
        arrived = lax.all_to_all(
            returned.reshape(n_space, CAP, tile_edge, slices),
            "space",
            split_axis=0,
            concat_axis=0,
            tiled=True,
        )
        slot_res = jnp.einsum(
            "ps,pik->sik",
            place_hot,
            arrived.reshape(n_space * CAP, tile_edge, slices),
            preferred_element_type=jnp.float32,
        ).astype(jnp.bfloat16)
        return (residual, slot_res)

    current = image
    pixels = lax.all_gather(current.astype(jnp.bfloat16), "angle", axis=0, tiled=True)
    for iteration in range(ITERS):
        blocks = pixels.reshape(block_count, tile_edge, slices)
        picked = jnp.take(blocks, block_ids, axis=0)
        products = jnp.einsum("tij,tjk->tik", tile_mats, picked, preferred_element_type=jnp.float32)
        gradient_partial_value = jnp.einsum(
            "ts,tik->sik", slot_hot, products, precision=lax.Precision.HIGHEST
        ).astype(jnp.bfloat16)
        gradient_residual, gradient_slot_res = ray_residual(gradient_partial_value)
        tile_res = jnp.take(gradient_slot_res, slot_ids, axis=0)
        back_terms = jnp.einsum(
            "tji,tjk->tik", tile_mats, tile_res, preferred_element_type=jnp.float32
        )
        block_terms = jnp.einsum(
            "tb,tik->bik", block_hot, back_terms, precision=lax.Precision.HIGHEST
        )
        grad_part = block_terms.reshape(block_count * tile_edge, slices)
        residual = gradient_residual
        gradient = lax.psum_scatter(
            grad_part.astype(jnp.bfloat16), "angle", scatter_dimension=0, tiled=True
        ).astype(jnp.float32)
        current = jnp.maximum(current - step_size * gradient, 0.0)
        if iteration + 1 < ITERS:
            pixels = lax.all_gather(current.astype(jnp.bfloat16), "angle", axis=0, tiled=True)
    return (current, residual[None])


def solution(mesh):
    placed = (
        P(("space", "angle"), None),
        P("space", "angle", None, None),
        P("space", "angle"),
        P("space", "angle"),
        P("space", "angle"),
        P("angle", "space", None, None),
        P("angle", "space", None, None),
    )
    return jax.shard_map(
        shards,
        mesh=mesh,
        in_specs=placed,
        out_specs=(P(("space", "angle"), None), P("angle", "space", None, None)),
        check_vma=False,
    )
```

profile of v0, /device:TPU:0, one launch (start us, length us, event | category | flops | bytes accessed | tf_op | source)
XLA Modules:
  0.0 358.6 jit_solution(15721778027608446314)
XLA Ops:
  7.2 1.8 convert_element_type.77
  11.3 4.2 %all-to-all-start = ((s32[4,1,2]{2,1,0:T(1,128)}), s32[4,1,2]{2,1,0:T(1,128)S(1)}, u32[]{:S(2)}, u32[]{:S(2)}) async-start(s32[4,1,2]{2,1,0:T(1,128)} %bitcast.8), calls=%async_computation | async-start | bytes 4096 | tf_op jit(solution)/shard_map/all_to_all | solution.py:43
  17.5 36.1 %all-gather.3.cloned.1.call-done = bf16[4096,128]{1,0:T(8,128)(2,1)} async-done(((bf16[512,128]{1,0:T(8,128)(2,1)}), bf16[4096,128]{1,0:T(8,128)(2,1)}) %all-gather.3.cloned.1.call-update) | async-done | bytes 1048592 | tf_op jit(solution)/shard_map/all_gather | solution.py:87
  53.6 4.0 %gather_fusion = bf16[96,128,128]{2,1,0:T(8,128)(2,1)} fusion(bf16[32,128,128]{2,1,0:T(8,128)(2,1)} %bitcast.110, s32[1024]{0:T(1024)S(1)} %pad_clamp_fusion.1), kind=kCustom, calls=%fused_computation.clone | custom fusion | bytes 6291840 | tf_op jit(solution)/shard_map/jit(_take)/gather | solution.py:90
  57.6 7.0 %fusion.16 = f32[96,128,128]{1,2,0:T(8,128)} fusion(bf16[1,96,128,128]{3,2,1,0:T(8,128)(2,1)S(1)} %copy-done, bf16[96,128,128]{2,1,0:T(8,128)(2,1)} %gather_fusion, pred[96]{0:T(512)(128)(4,1)S(1)} %compare_and_fusion.1), kind=kOutput, calls=%fused_computation.20 | convolution fusion | flops 404226048 | bytes 12583008 | tf_op jit(solution)/shard_map/tij,tjk->tik/dot_general | solution.py:91
  64.6 6.7 %copy.68 = f32[96,128,128]{2,0,1:T(8,128)} copy(f32[96,128,128]{1,2,0:T(8,128)} %fusion.16) | data formatting | bytes 12582912 | tf_op jit(solution)/shard_map/tij,tjk->tik/dot_general | solution.py:91
  71.3 4.9 %convolution_convert_fusion.3 = bf16[8,128,128]{2,0,1:T(8,128)(2,1)S(1)} fusion(f32[96,128,128]{2,0,1:T(8,128)} %copy.68, s32[96]{0:T(128)S(1)} %bitcast.123), kind=kOutput, calls=%fused_computation.31 | convolution fusion | flops 151126784 | bytes 6553984 | tf_op jit(solution)/shard_map/ts,tik->sik/dot_general | solution.py:92
  77.4 3.4 all-to-all-start.1
  81.0 5.9 %all-to-all-done.1 = bf16[4,2,128,128]{3,1,2,0:T(2,128)(2,1)S(1)} async-done(((bf16[4,2,128,128]{3,1,2,0:T(2,128)(2,1)}), bf16[4,2,128,128]{3,1,2,0:T(2,128)(2,1)S(1)}, u32[]{:S(2)}, u32[]{:S(2)}) %all-to-all-start.1) | async-done | bytes 262176 | tf_op jit(solution)/shard_map/all_to_all | solution.py:54
  87.7 1.5 convolution_convert_fusion.9
  90.1 3.4 all-to-all-start.2
  93.7 5.8 %all-to-all-done.2 = bf16[4,2,128,128]{3,1,2,0:T(2,128)(2,1)S(1)} async-done(((bf16[4,2,128,128]{3,1,2,0:T(2,128)(2,1)}), bf16[4,2,128,128]{3,1,2,0:T(2,128)(2,1)S(1)}, u32[]{:S(2)}, u32[]{:S(2)}) %all-to-all-start.2) | async-done | bytes 262176 | tf_op jit(solution)/shard_map/all_to_all | solution.py:71
  100.0 2.8 gather_fusion.1
  102.8 5.9 %fusion.21 = f32[96,128,128]{1,2,0:T(8,128)} fusion(bf16[1,96,128,128]{3,2,1,0:T(8,128)(2,1)S(1)} %copy-done, bf16[96,128,128]{2,1,0:T(8,128)(2,1)} %gather_fusion.1, pred[96]{0:T(512)(128)(4,1)S(1)} %compare_and_fusion), kind=kOutput, calls=%fused_computation.21 | convolution fusion | flops 404226048 | bytes 12583008 | tf_op jit(solution)/shard_map/tji,tjk->tik/dot_general | solution.py:97
  108.6 6.7 %copy.77 = f32[96,128,128]{2,0,1:T(8,128)} copy(f32[96,128,128]{1,2,0:T(8,128)} %fusion.21) | data formatting | bytes 12582912 | tf_op jit(solution)/shard_map/tji,tjk->tik/dot_general | solution.py:97
  115.3 5.2 %convolution_convert_fusion.1 = bf16[32,128,128]{2,0,1:T(8,128)(2,1)S(1)} fusion(f32[96,128,128]{2,0,1:T(8,128)} %copy.77, s32[96]{0:T(128)S(1)} %bitcast.125), kind=kOutput, calls=%fused_computation.29 | convolution fusion | flops 604507136 | bytes 7340416 | tf_op jit(solution)/shard_map/tb,tik->bik/dot_general | solution.py:100
  120.5 1.4 copy.78
  122.0 61.3 %reduce-scatter.3.cloned.1.call-done = bf16[512,128]{1,0:T(8,128)(2,1)} async-done(((bf16[4096,128]{1,0:T(8,128)(2,1)}), bf16[512,128]{1,0:T(8,128)(2,1)}) %reduce-scatter.3.cloned.1.call-update) | async-done | bytes 131088 | tf_op jit(solution)/shard_map/reduce_scatter | solution.py:105
  183.3 1.6 fusion.46
  185.0 40.5 %all-gather.5.cloned.1.call-done = bf16[4096,128]{1,0:T(8,128)(2,1)} async-done(((bf16[512,128]{1,0:T(8,128)(2,1)}), bf16[4096,128]{1,0:T(8,128)(2,1)}) %all-gather.5.cloned.1.call-update) | async-done | bytes 1048592 | tf_op jit(solution)/shard_map/all_gather | solution.py:110
  225.4 4.0 %gather_fusion.2 = bf16[96,128,128]{2,1,0:T(8,128)(2,1)} fusion(bf16[32,128,128]{2,1,0:T(8,128)(2,1)} %bitcast.111, s32[1024]{0:T(1024)S(1)} %pad_clamp_fusion.1), kind=kCustom, calls=%fused_computation.2.clone | custom fusion | bytes 6291840 | tf_op jit(solution)/shard_map/jit(_take)/gather | solution.py:90
  229.4 7.0 %fusion.26 = f32[96,128,128]{1,2,0:T(8,128)} fusion(bf16[1,96,128,128]{3,2,1,0:T(8,128)(2,1)S(1)} %copy-done, bf16[96,128,128]{2,1,0:T(8,128)(2,1)} %gather_fusion.2, pred[96]{0:T(512)(128)(4,1)S(1)} %compare_and_fusion.1), kind=kOutput, calls=%fused_computation.22 | convolution fusion | flops 404226048 | bytes 12583008 | tf_op jit(solution)/shard_map/tij,tjk->tik/dot_general | solution.py:91
  236.4 6.7 %copy.80 = f32[96,128,128]{2,0,1:T(8,128)} copy(f32[96,128,128]{1,2,0:T(8,128)} %fusion.26) | data formatting | bytes 12582912 | tf_op jit(solution)/shard_map/tij,tjk->tik/dot_general | solution.py:91
  243.1 5.0 %convolution_convert_fusion.2 = bf16[8,128,128]{2,0,1:T(8,128)(2,1)S(1)} fusion(f32[96,128,128]{2,0,1:T(8,128)} %copy.80, s32[96]{0:T(128)S(1)} %bitcast.124), kind=kOutput, calls=%fused_computation.30 | convolution fusion | flops 151126784 | bytes 6553984 | tf_op jit(solution)/shard_map/ts,tik->sik/dot_general | solution.py:92
  248.6 8.6 %all_to_all.29 = bf16[4,2,128,128]{3,1,2,0:T(2,128)(2,1)S(1)} all-to-all(bf16[4,2,128,128]{3,1,2,0:T(2,128)(2,1)S(1)} %copy.82), channel_id=1, replica_groups=mesh['space'=4,'angle'=8] {'space'}, dimensions={0} | all-to-all | bytes 524288 | tf_op jit(solution)/shard_map/all_to_all | solution.py:54
  258.1 8.4 %all_to_all.30 = bf16[4,2,128,128]{3,1,2,0:T(2,128)(2,1)S(1)} all-to-all(bf16[4,2,128,128]{3,1,2,0:T(2,128)(2,1)S(1)} %copy.84), channel_id=1, replica_groups=mesh['space'=4,'angle'=8] {'space'}, dimensions={0} | all-to-all | bytes 524288 | tf_op jit(solution)/shard_map/all_to_all | solution.py:71
  267.0 2.8 gather_fusion.3
  269.8 5.9 %fusion.31 = f32[96,128,128]{1,2,0:T(8,128)} fusion(bf16[1,96,128,128]{3,2,1,0:T(8,128)(2,1)S(1)} %copy-done, bf16[96,128,128]{2,1,0:T(8,128)(2,1)} %gather_fusion.3, pred[96]{0:T(512)(128)(4,1)S(1)} %compare_and_fusion), kind=kOutput, calls=%fused_computation.23 | convolution fusion | flops 404226048 | bytes 12583008 | tf_op jit(solution)/shard_map/tji,tjk->tik/dot_general | solution.py:97
  275.7 6.7 %copy.88 = f32[96,128,128]{2,0,1:T(8,128)} copy(f32[96,128,128]{1,2,0:T(8,128)} %fusion.31) | data formatting | bytes 12582912 | tf_op jit(solution)/shard_map/tji,tjk->tik/dot_general | solution.py:97
  282.3 5.2 %convolution_convert_fusion = bf16[32,128,128]{2,0,1:T(8,128)(2,1)S(1)} fusion(f32[96,128,128]{2,0,1:T(8,128)} %copy.88, s32[96]{0:T(128)S(1)} %bitcast.126), kind=kOutput, calls=%fused_computation.28 | convolution fusion | flops 604507136 | bytes 7340416 | tf_op jit(solution)/shard_map/tb,tik->bik/dot_general | solution.py:100
  289.6 60.7 %reduce-scatter.5.cloned.1.call-done = bf16[512,128]{1,0:T(8,128)(2,1)} async-done(((bf16[4096,128]{1,0:T(8,128)(2,1)}), bf16[512,128]{1,0:T(8,128)(2,1)}) %reduce-scatter.5.cloned.1.call-update) | async-done | bytes 131088 | tf_op jit(solution)/shard_map/reduce_scatter | solution.py:105
  350.4 1.7 subtract_maximum_fusion
  (58 shorter events, 12.3 us)
Async XLA Ops:
  7.2 50.4 %copy-start = (bf16[1,96,128,128]{3,2,1,0:T(8,128)(2,1)S(1)}, bf16[1,96,128,128]{3,2,1,0:T(8,128)(2,1)}, u32[]{:S(2)}) copy-start(bf16[1,96,128,128]{3,2,1,0:T(8,128)(2,1)} %param.12) | copy-start | bytes 9437188
  7.2 46.4 %all-gather.3.cloned.1.call-start = ((), (), s32[]{:S(2)}) async-start(), calls=%async_computation.7 | async-start | bytes 1179648 | tf_op jit(solution)/shard_map/all_gather | solution.py:87
  11.3 66.1 %all-to-all-start = ((s32[4,1,2]{2,1,0:T(1,128)}), s32[4,1,2]{2,1,0:T(1,128)S(1)}, u32[]{:S(2)}, u32[]{:S(2)}) async-start(s32[4,1,2]{2,1,0:T(1,128)} %bitcast.8), calls=%async_computation | async-start | bytes 4096 | tf_op jit(solution)/shard_map/all_to_all | solution.py:43
  64.6 6.7 %copy-start.3 = (s32[1,96]{1,0:T(1,128)S(1)}, s32[1,96]{1,0:T(1,128)}, u32[]{:S(2)}) copy-start(s32[1,96]{1,0:T(1,128)} %param.13) | copy-start | bytes 1156
  77.4 9.4 %all-to-all-start.1 = ((bf16[4,2,128,128]{3,1,2,0:T(2,128)(2,1)}), bf16[4,2,128,128]{3,1,2,0:T(2,128)(2,1)S(1)}, u32[]{:S(2)}, u32[]{:S(2)}) async-start(bf16[4,2,128,128]{3,1,2,0:T(2,128)(2,1)} %copy.70), calls=%async_computation.1 | async-start | bytes 524288 | tf_op jit(solution)/shard_map/all_to_all | solution.py:54
  90.1 9.4 %all-to-all-start.2 = ((bf16[4,2,128,128]{3,1,2,0:T(2,128)(2,1)}), bf16[4,2,128,128]{3,1,2,0:T(2,128)(2,1)S(1)}, u32[]{:S(2)}, u32[]{:S(2)}) async-start(bf16[4,2,128,128]{3,1,2,0:T(2,128)(2,1)} %copy.73), calls=%async_computation.2 | async-start | bytes 524288 | tf_op jit(solution)/shard_map/all_to_all | solution.py:71
  93.5 89.8 %reduce-scatter.3.cloned.1.call-start = ((), (), s32[]{:S(2)}) async-start(), calls=%async_computation.8 | async-start | bytes 1179648 | tf_op jit(solution)/shard_map/reduce_scatter | solution.py:105
  108.6 6.7 %copy-start.4 = (s32[1,96]{1,0:T(1,128)S(1)}, s32[1,96]{1,0:T(1,128)}, u32[]{:S(2)}) copy-start(s32[1,96]{1,0:T(1,128)} %param.14) | copy-start | bytes 1156
  120.5 62.8 %copy-start.1 = (f32[512,128]{1,0:T(8,128)S(1)}, f32[512,128]{1,0:T(8,128)}, u32[]{:S(2)}) copy-start(f32[512,128]{1,0:T(8,128)} %param.11) | copy-start | bytes 786436
  121.9 103.5 %all-gather.5.cloned.1.call-start = ((), (), s32[]{:S(2)}) async-start(), calls=%async_computation.9 | async-start | bytes 1179648 | tf_op jit(solution)/shard_map/all_gather | solution.py:110
  184.9 165.5 %reduce-scatter.5.cloned.1.call-start = ((), (), s32[]{:S(2)}) async-start(), calls=%async_computation.10 | async-start | bytes 1179648 | tf_op jit(solution)/shard_map/reduce_scatter | solution.py:105
  243.1 14.3 %copy-start.6 = (bf16[1,4,128,128]{3,2,1,0:T(8,128)(2,1)S(1)}, bf16[1,4,128,128]{3,2,1,0:T(8,128)(2,1)}, u32[]{:S(2)}) copy-start(bf16[1,4,128,128]{3,2,1,0:T(8,128)(2,1)} %param.16) | copy-start | bytes 393220
  243.1 14.3 %copy-start.7 = (bf16[1,4,128,128]{3,2,1,0:T(8,128)(2,1)S(1)}, bf16[1,4,128,128]{3,2,1,0:T(8,128)(2,1)}, u32[]{:S(2)}) copy-start(bf16[1,4,128,128]{3,2,1,0:T(8,128)(2,1)} %param.17) | copy-start | bytes 393220
  275.7 6.7 %copy-start.5 = (s32[1,96]{1,0:T(1,128)S(1)}, s32[1,96]{1,0:T(1,128)}, u32[]{:S(2)}) copy-start(s32[1,96]{1,0:T(1,128)} %param.14) | copy-start | bytes 1156
  287.6 62.8 %copy-start.2 = (f32[512,128]{1,0:T(8,128)S(1)}, f32[512,128]{1,0:T(8,128)}, u32[]{:S(2)}) copy-start(f32[512,128]{1,0:T(8,128)} %param.11) | copy-start | bytes 786436
Sparse Core Ops, SparseCore 0:
  10.7 42.8 all-gather.2
  122.0 61.1 reduce-scatter.2
  186.2 39.1 all-gather.4
  289.1 61.2 reduce-scatter.4
where the time goes:
time: 360 us; the launch traced here: 359 us
  waiting for transfers between devices  210 us (58%)
  matrix products  49.3 us (14%)
  local copies, waits for them, and re-layouts  48 us (13%)
  blocking collectives  17 us (5%)
  between operations  13.9 us (4%)
  starting transfers between devices  11.4 us (3%)
  other arithmetic  8.77 us (2%)
    reduce_scatter x2, waiting for transfers between devices, shards(): lax.psum_scatter(grad_part.astype(jnp.bfloat16), 'angle', scatter_dimensi...  122 us
    all_gather x2, waiting for transfers between devices, shards(): lax.all_gather(current.astype(jnp.bfloat16), 'angle', axis=0, tiled=True)  76.5 us
    dot_general x2, matrix products, shards(): jnp.einsum('tij,tjk->tik', tile_mats, picked, preferred_element_type=jnp....  14 us
    dot_general x2, local copies, waits for them, and re-layouts, shards(): jnp.einsum('tji,tjk->tik', tile_mats, tile_res, preferred_element_type=jn...  13.3 us
    dot_general x2, local copies, waits for them, and re-layouts, shards(): jnp.einsum('tij,tjk->tik', tile_mats, picked, preferred_element_type=jnp....  13.3 us
    dot_general x2, matrix products, shards(): jnp.einsum('tji,tjk->tik', tile_mats, tile_res, preferred_element_type=jn...  11.7 us
    dot_general x2, matrix products, shards(): jnp.einsum('tb,tik->bik', block_hot, back_terms, precision=lax.Precision....  10.4 us
    dot_general x2, matrix products, shards(): jnp.einsum('ts,tik->sik', slot_hot, products, precision=lax.Precision.HIG...  9.87 us
  transfers between devices with their start and end apart: 7, of which 6 were waited for; matrix products, arithmetic and copies ran while one was open for 8% of the time, Pallas kernels for 0%

commit v1 on v0

v1 whole, which is shorter than its diff:
```python
import functools
import math

import jax
import jax.numpy as jnp
from jax import lax
from jax.experimental import pallas as pl
from jax.experimental.pallas import tpu as pltpu
from jax.sharding import PartitionSpec as P

CAP = 2
ITERS = 2
MESH = pl.DeviceIdType.MESH
F32 = jnp.float32
BF16 = jnp.bfloat16


def kernel(
    dims, image, tiles, slot_row, block_row, ray_list, sinogram, weights, volume, residual,
    tile_v, run_f, run_t, mat, mat_t, pix, acc, part, ray_in, ray_res, ray_out, slot_res,
    grad_out, grad_in, chain_out, chain_dn, chain_up, key_v, table_v, table_s, ids_out, ids_in,
    ids_s, local_sem, ag_send, ag_recv, id_send, id_recv, ray_send, ray_recv, back_send,
    back_recv, gx_send, gx_recv, dn_send, dn_recv, up_send, up_recv,
):
    n_space, n_angle, nx, nz, edge, own, slots, step_size = dims
    count = tiles.shape[0]
    width = key_v.shape[1]
    share = image.shape[0]
    per_chunk = share // edge
    blocks = per_chunk * n_angle
    seats = n_space * CAP
    me_s = lax.axis_index("space")
    me_a = lax.axis_index("angle")
    z, x = me_a // nx, me_a % nx
    has_up, has_dn = z < nz - 1, z > 0
    x_peers = [(x + j) % nx for j in range(1, nx)]
    s_peers = [(me_s + j) % n_space for j in range(1, n_space)]

    def at_angle(zz, xx):
        return (me_s, zz * nx + xx)

    def remote(src, dst, send, recv, device):
        return pltpu.make_async_remote_copy(
            src_ref=src, dst_ref=dst, send_sem=send, recv_sem=recv, device_id=device,
            device_id_type=MESH,
        )

    barrier = pltpu.get_barrier_semaphore()

    def greet(device):
        pl.semaphore_signal(barrier, inc=1, device_id=device, device_id_type=MESH)

    @pl.when(has_up)
    def _():
        greet(at_angle(z + 1, x))

    @pl.when(has_dn)
    def _():
        greet(at_angle(z - 1, x))

    for xx in x_peers:
        greet(at_angle(z, xx))
    for ss in s_peers:
        greet((ss, me_a))
    tile_copy = pltpu.make_async_copy(tiles, tile_v.at[pl.ds(0, count)], local_sem.at[0])
    tile_copy.start()
    volume[...] = image[...]
    pix[me_a] = image[...].astype(BF16)
    friends = has_up.astype(jnp.int32) + has_dn.astype(jnp.int32) + (nx - 1 + n_space - 1)
    pl.semaphore_wait(barrier, friends)

    def ag_copy(kind, src_a, device):
        return remote(
            pix.at[src_a], pix.at[src_a], ag_send.at[kind, src_a], ag_recv.at[src_a], device
        )

    def ag_copies(src_z, go_up, go_dn):
        src_a = src_z * nx + x
        listed = []
        if go_up:
            listed.append((has_up, ag_copy(0, src_a, at_angle(jnp.minimum(z + 1, nz - 1), x))))
        if go_dn:
            listed.append((has_dn, ag_copy(1, src_a, at_angle(jnp.maximum(z - 1, 0), x))))
        for j, xx in enumerate(x_peers):
            listed.append((None, ag_copy(2 + j, src_a, at_angle(z, xx))))
        return listed

    def each(listed, act):
        for cond, copy in listed:
            if cond is None:
                act(copy)
            else:
                pl.when(cond)(functools.partial(act, copy))

    def start(copy):
        copy.start()

    def wait_send(copy):
        copy.wait_send()

    def ag_wait(src_a):
        ag_copy(0, src_a, (me_s, me_a)).wait_recv()

    def gather(work):
        each(ag_copies(z, True, True), start)
        work(0)
        for k in range(1, nz):

            @pl.when(z - k >= 0)
            def _():
                ag_wait((z - k) * nx + x)
                each(ag_copies(z - k, True, False), start)

            @pl.when(z + k < nz)
            def _():
                ag_wait((z + k) * nx + x)
                each(ag_copies(z + k, False, True), start)

            work(k)

    def gather_end():
        each(ag_copies(z, True, True), wait_send)
        for k in range(1, nz):

            @pl.when(z - k >= 0)
            def _():
                each(ag_copies(z - k, True, False), wait_send)

            @pl.when(z + k < nz)
            def _():
                each(ag_copies(z + k, False, True), wait_send)

    def prepare():
        rays = [ray_list[0, j] for j in range(slots)]
        owners = [r // own for r in rays]
        seat = []
        for j in range(slots):
            rank = jnp.int32(0)
            for i in range(j):
                rank = rank + (owners[i] == owners[j]).astype(jnp.int32)
            seat.append(owners[j] * CAP + rank)
        for p in range(seats):
            local = jnp.int32(-1)
            for j in range(slots):
                local = jnp.where(seat[j] == p, rays[j] % own, local)
            ids_out[p // CAP, p % CAP, :] = jnp.full((128,), local, jnp.int32)
        ids_in[me_s] = ids_out[me_s]
        for j, ss in enumerate(s_peers):
            remote(
                ids_out.at[ss], ids_in.at[me_s], id_send.at[j], id_recv.at[me_s], (ss, me_a)
            ).start()
        spread = jnp.zeros((1, count), jnp.int32)
        for j in range(slots):
            spread = jnp.where(slot_row[...] == j, seat[j], spread)
        key_v[...] = jnp.full(key_v.shape, -1, jnp.int32)
        key_v[0:1, 0:count] = spread * blocks + block_row[...]
        across = jnp.broadcast_to(key_v[0:1, :], (width, width))
        down = across.T
        u = lax.broadcasted_iota(jnp.int32, (width, width), 0)
        t = lax.broadcasted_iota(jnp.int32, (width, width), 1)
        before = jnp.max(jnp.where((across == down) & (u < t), u, -1), axis=0, keepdims=True)
        table_v[0:1, :] = jnp.where(before < 0, count, before)
        for j in range(-(-seats * blocks // width)):
            last = jnp.max(jnp.where(down == t + j * width, u, -1), axis=0, keepdims=True)
            table_v[1 + j : 2 + j, :] = jnp.where(last < 0, count, last)
        copy = pltpu.make_async_copy(table_v, table_s, local_sem.at[1])
        copy.start()
        copy.wait()
        run_f[count] = jnp.zeros((edge, edge), F32)
        run_t[count] = jnp.zeros((edge, edge), BF16)
        tile_copy.wait()
        tile_v[count] = jnp.zeros((edge, edge), BF16)

    def run_tiles(begin, end):
        @pl.loop(begin, end)
        def _(t):
            total = tile_v[t].astype(F32) + run_f[table_s[0, t]]
            run_f[t] = total
            tile_v[t] = total.astype(BF16)
            run_t[t] = total.T.astype(BF16)

    def build(begin, end):
        @pl.loop(begin, end)
        def _(c):
            for p in range(seats):
                for q in range(per_chunk):
                    cell = p * blocks + c * per_chunk + q
                    which = table_s[1 + cell // width, cell % width]
                    mat[c, p * edge : (p + 1) * edge, q * edge : (q + 1) * edge] = tile_v[which]
                    mat_t[c, q * edge : (q + 1) * edge, p * edge : (p + 1) * edge] = run_t[which]

    def project(c):
        acc[0 : seats * edge] += jnp.dot(mat[c], pix[c], preferred_element_type=F32)

    def first_work(k):
        half = count // 2
        if k == 0:
            prepare()
            run_tiles(0, half)
        if k == min(1, nz - 1):
            run_tiles(half, count)
        if k == min(2, nz - 1):
            build(0, n_angle)

    def across_x(src_z):
        for xx in x_peers:
            ag_wait(src_z * nx + xx)
            project(src_z * nx + xx)

    def later_work(k):
        if k == 0:
            acc[...] = jnp.zeros(acc.shape, F32)
            project(me_a)
            return

        @pl.when(z - k >= 0)
        def _():
            project((z - k) * nx + x)

        @pl.when(z + k < nz)
        def _():
            project((z + k) * nx + x)

        if k == 1:
            across_x(z)
        else:

            @pl.when(z - k + 1 >= 0)
            def _():
                across_x(z - k + 1)

            @pl.when(z + k - 1 < nz)
            def _():
                across_x(z + k - 1)

    def later_end():
        k = nz - 1

        @pl.when(z - k >= 0)
        def _():
            across_x(z - k)

        @pl.when(z + k < nz)
        def _():
            across_x(z + k)

    def first_end():
        acc[...] = jnp.zeros(acc.shape, F32)
        for zz in range(nz):
            for xx in x_peers:
                ag_wait(zz * nx + xx)

        @pl.loop(0, n_angle)
        def _(c):
            project(c)

    group = CAP * edge

    def ray_copy(j, ss):
        return remote(
            part.at[pl.ds(ss * CAP, CAP)], ray_in.at[pl.ds(me_s * CAP, CAP)],
            ray_send.at[j], ray_recv.at[me_s], (ss, me_a),
        )

    def ray_wait(ss):
        rows = pl.ds(ss * CAP, CAP)
        remote(
            part.at[rows], ray_in.at[rows], ray_send.at[0], ray_recv.at[ss], (ss, me_a)
        ).wait_recv()

    def back_copy(j, ss):
        return remote(
            ray_out.at[pl.ds(ss * group, group)], slot_res.at[pl.ds(me_s * group, group)],
            back_send.at[j], back_recv.at[me_s], (ss, me_a),
        )

    def back_wait(ss):
        rows = pl.ds(ss * group, group)
        remote(
            ray_out.at[rows], slot_res.at[rows], back_send.at[0], back_recv.at[ss], (ss, me_a)
        ).wait_recv()

    def exchange(first):
        part[...] = acc[0 : seats * edge].astype(BF16).reshape(part.shape)
        for j, ss in enumerate(s_peers):
            ray_copy(j, ss).start()
        mine = pl.ds(me_s * CAP, CAP)
        ray_in[mine] = part[mine]
        if first:
            ray_in[seats] = jnp.zeros((edge, edge), BF16)
            ray_res[own] = jnp.zeros((edge, edge), BF16)
            for j, ss in enumerate(s_peers):
                copy = remote(
                    ids_out.at[ss], ids_in.at[ss], id_send.at[j], id_recv.at[ss], (ss, me_a)
                )
                copy.wait_send()
                copy.wait_recv()
            copy = pltpu.make_async_copy(ids_in, ids_s, local_sem.at[1])
            copy.start()
            copy.wait()
        for ss in s_peers:
            ray_wait(ss)
        for o in range(own):
            total = -sinogram[o].astype(F32)
            for ss in range(n_space):
                where = jnp.int32(seats)
                for c in range(CAP):
                    where = jnp.where(ids_s[ss, c, 0] == o, ss * CAP + c, where)
                total = total + ray_in[where].astype(F32)
            ray_res[o] = (weights[o].astype(F32) * total).astype(BF16)
        for j, ss in enumerate(s_peers):
            for c in range(CAP):
                which = ids_s[ss, c, 0]
                which = jnp.where(which < 0, own, which)
                ray_out[pl.ds(ss * group + c * edge, edge)] = ray_res[which]
            back_copy(j, ss).start()
        for c in range(CAP):
            which = ids_s[me_s, c, 0]
            which = jnp.where(which < 0, own, which)
            slot_res[pl.ds(me_s * group + c * edge, edge)] = ray_res[which]
        for ss in s_peers:
            back_wait(ss)

    def exchange_end():
        for j, ss in enumerate(s_peers):
            ray_copy(j, ss).wait_send()
            back_copy(j, ss).wait_send()

    def gx_copy(dst_z, j, xx):
        return remote(
            grad_out.at[dst_z, j], grad_in.at[dst_z, j], gx_send.at[dst_z, j],
            gx_recv.at[dst_z, j], at_angle(z, xx),
        )

    def dn_copy(dst_z):
        return remote(
            chain_out.at[dst_z], chain_dn.at[dst_z], dn_send.at[dst_z], dn_recv.at[dst_z],
            at_angle(jnp.maximum(z - 1, 0), x),
        )

    def up_copy(dst_z):
        return remote(
            chain_out.at[dst_z], chain_up.at[dst_z], up_send.at[dst_z], up_recv.at[dst_z],
            at_angle(jnp.minimum(z + 1, nz - 1), x),
        )

    def back(c):
        return jnp.dot(mat_t[c], slot_res[...], preferred_element_type=F32)

    def send_terms(dst_z):
        for j, xx in enumerate(x_peers):
            grad_out[dst_z, j] = back(dst_z * nx + xx).astype(BF16)
            gx_copy(dst_z, j, xx).start()

    def sum_terms(dst_z):
        acc[0:share] = back(dst_z * nx + x)
        for j in range(nx - 1):
            gx_copy(dst_z, j, x_peers[j]).wait_recv()
            acc[0:share] += grad_in[dst_z, j].astype(F32)

    def add_dn(dst_z):
        dn_copy(dst_z).wait_recv()
        acc[0:share] += chain_dn[dst_z].astype(F32)

    def add_up(dst_z):
        up_copy(dst_z).wait_recv()
        acc[0:share] += chain_up[dst_z].astype(F32)

    def scatter():
        for k in range(nz - 1, 0, -1):

            @pl.when(z - k >= 0)
            def _():
                send_terms(z - k)

            @pl.when(z + k < nz)
            def _():
                send_terms(z + k)

        send_terms(z)
        for k in range(nz - 1, 0, -1):

            @pl.when(z - k >= 0)
            def _():
                sum_terms(z - k)
                pl.when(has_up)(functools.partial(add_dn, z - k))
                chain_out[z - k] = acc[0:share].astype(BF16)
                dn_copy(z - k).start()

            @pl.when(z + k < nz)
            def _():
                sum_terms(z + k)
                pl.when(has_dn)(functools.partial(add_up, z + k))
                chain_out[z + k] = acc[0:share].astype(BF16)
                up_copy(z + k).start()

        sum_terms(z)
        pl.when(has_up)(functools.partial(add_dn, z))
        pl.when(has_dn)(functools.partial(add_up, z))
        volume[...] = jnp.maximum(volume[...] - step_size * acc[0:share], 0.0)

    def scatter_end():
        for dst_z in range(nz):
            for j, xx in enumerate(x_peers):
                gx_copy(dst_z, j, xx).wait_send()

            @pl.when(z > dst_z)
            def _():
                dn_copy(dst_z).wait_send()

            @pl.when(z < dst_z)
            def _():
                up_copy(dst_z).wait_send()

    for iteration in range(ITERS):
        if iteration == 0:
            gather(first_work)
            first_end()
        else:
            pix[me_a] = volume[...].astype(BF16)
            gather(later_work)
            later_end()
        exchange(iteration == 0)
        gather_end()
        scatter()
        exchange_end()
        scatter_end()
    residual[...] = ray_res[0:own]


def shards(image, tiles, tile_slot, tile_block, slot_ray, sinogram, weights):
    n_space = lax.axis_size("space")
    n_angle = lax.axis_size("angle")
    tile_mats = tiles[0]
    count, edge = tile_mats.shape[:2]
    slices = image.shape[1]
    share = image.shape[0]
    own = sinogram.shape[1]
    slots = slot_ray.shape[1]
    blocks = share * n_angle // edge
    seats = n_space * CAP
    nx = max(1, math.isqrt(n_angle // 2))
    while n_angle % nx:
        nx -= 1
    nz = n_angle // nx
    width = -(-count // 128) * 128
    table = -(-(1 + -(-seats * blocks // width)) // 8) * 8
    step_size = 0.2 * math.sqrt(blocks / (n_angle * own))
    dims = (n_space, n_angle, nx, nz, edge, own, slots, step_size)
    vmem, dma = pltpu.VMEM, pltpu.SemaphoreType.DMA
    others, sides = n_space - 1, nx - 1
    whole = pl.BlockSpec(memory_space=pltpu.VMEM)
    volume, residual = pl.pallas_call(
        functools.partial(kernel, dims),
        out_shape=(
            jax.ShapeDtypeStruct((share, slices), F32),
            jax.ShapeDtypeStruct((own, edge, slices), BF16),
        ),
        in_specs=[
            whole, pl.BlockSpec(memory_space=pl.ANY), whole, whole,
            pl.BlockSpec(memory_space=pltpu.SMEM), whole, whole,
        ],
        out_specs=(whole, whole),
        scratch_shapes=[
            vmem((count + 1, edge, edge), BF16),
            vmem((count + 1, edge, edge), F32),
            vmem((count + 1, edge, edge), BF16),
            vmem((n_angle, seats * edge, share), BF16),
            vmem((n_angle, share, seats * edge), BF16),
            vmem((n_angle, share, slices), BF16),
            vmem((max(seats * edge, share), slices), F32),
            vmem((seats, edge, slices), BF16),
            vmem((seats + 1, edge, slices), BF16),
            vmem((own + 1, edge, slices), BF16),
            vmem((seats * edge, slices), BF16),
            vmem((seats * edge, slices), BF16),
            vmem((nz, sides, share, slices), BF16),
            vmem((nz, sides, share, slices), BF16),
            vmem((nz, share, slices), BF16),
            vmem((nz, share, slices), BF16),
            vmem((nz, share, slices), BF16),
            vmem((8, width), jnp.int32),
            vmem((table, width), jnp.int32),
            pltpu.SMEM((table, width), jnp.int32),
            vmem((n_space, 8, 128), jnp.int32),
            vmem((n_space, 8, 128), jnp.int32),
            pltpu.SMEM((n_space, 8, 128), jnp.int32),
            dma((2,)),
            dma((2 + sides, n_angle)), dma((n_angle,)),
            dma((others,)), dma((n_space,)),
            dma((others,)), dma((n_space,)),
            dma((others,)), dma((n_space,)),
            dma((nz, sides)), dma((nz, sides)),
            dma((nz,)), dma((nz,)),
            dma((nz,)), dma((nz,)),
        ],
        compiler_params=pltpu.CompilerParams(
            collective_id=0, has_side_effects=True, vmem_limit_bytes=58 * 1024 * 1024
        ),
    )(image, tile_mats, tile_slot, tile_block, slot_ray, sinogram[0], weights[0])
    return (volume, residual[None])


def solution(mesh):
    placed = (
        P(("space", "angle"), None),
        P("space", "angle", None, None),
        P("space", "angle"),
        P("space", "angle"),
        P("space", "angle"),
        P("angle", "space", None, None),
        P("angle", "space", None, None),
    )
    return jax.shard_map(
        shards,
        mesh=mesh,
        in_specs=placed,
        out_specs=(P(("space", "angle"), None), P("angle", "space", None, None)),
        check_vma=False,
    )
```

time: 360 us -> 107 us (0.30)
  waiting for transfers between devices: 210 us -> 0 us
  Pallas kernels: 0 us -> 103 us
  matrix products: 49.3 us -> 0 us
  local copies, waits for them, and re-layouts: 48 us -> 3.24 us
  blocking collectives: 17 us -> 0 us
  between operations: 13.9 us -> 0.64 us
  starting transfers between devices: 11.4 us -> 0 us
  other arithmetic: 8.77 us -> 0 us
    reduce_scatter x2 -> x0, waiting for transfers between devices: 122 us -> none  [shards(): lax.psum_scatter(grad_part.astype(jnp.bfloat16), 'angle', scatter_dimensi...]
    pallas_call x0 -> x1, Pallas kernels: none -> 103 us  [shards(): pl.pallas_call(functools.partial(kernel, dims), out_shape=(jax.ShapeDtype...]
    all_gather x2 -> x0, waiting for transfers between devices: 76.5 us -> none  [shards(): lax.all_gather(current.astype(jnp.bfloat16), 'angle', axis=0, tiled=True)]
    dot_general x15 -> x0, matrix products: 49.3 us -> none  [the longest x2 14 us: shards(): jnp.einsum('tij,tjk->tik', tile_mats, picked, preferred_element_type=jnp....]
    dot_general x4 -> x0, local copies, waits for them, and re-layouts: 26.7 us -> none  [the longest x2 13.3 us: shards(): jnp.einsum('tji,tjk->tik', tile_mats, tile_res, preferred_element_type=jn...]
    all_to_all x2 -> x0, blocking collectives: 17 us -> none  [the longest x1 8.58 us: ray_residual(): lax.all_to_all(outgoing.reshape(n_space, CAP, tile_edge, slices), 'space'...]
    gather x4 -> x0, local copies, waits for them, and re-layouts: 13.5 us -> none  [the longest x2 7.96 us: shards(): picked = jnp.take(blocks, block_ids, axis=0)]
    all_to_all x3 -> x0, waiting for transfers between devices: 11.6 us -> none  [the longest x1 5.88 us: ray_residual(): lax.all_to_all(outgoing.reshape(n_space, CAP, tile_edge, slices), 'space'...]
  transfers between devices with their start and end apart: 7 -> 0, of which waited for: 6 -> 0; matrix products, arithmetic and copies ran while one was open for 8% -> 0% of each run, Pallas kernels for 0% -> 0%
where the time goes in v1:
time: 107 us
  Pallas kernels  103 us (96%)
  local copies, waits for them, and re-layouts  3.24 us (3%)
    pallas_call x1, Pallas kernels, shards(): pl.pallas_call(functools.partial(kernel, dims), out_shape=(jax.ShapeDtype...  103 us
    unnamed x2, local copies, waits for them, and re-layouts  3.24 us

profile of v1, /device:TPU:0, one launch (start us, length us, event | category | flops | bytes accessed | tf_op | source)
XLA Modules:
  0.0 106.8 jit_solution(6553937637376231252)
XLA Ops:
  0.6 103.0 %shard_map.86 = (f32[512,128]{1,0:T(8,128)}, bf16[4,128,128]{2,1,0:T(8,128)(2,1)}) custom-call(f32[512,128]{1,0:T(8,128)} %image.1, bf16[96,128,128]{2,1,0:T(8,128)(2,1)} %bitcast.4, s32[1,96]{1,0:T(1,128)} %slot_row.1, s32[1,96]{1,0:T(1,128)} %block_row.1, s32[1,8]{1,0:T(1,128)} %ray_list.1, bf16[4,128,128]{2,1,0:T(8,128)(2,1)} %bitcast.5, ...), custom_call_target="tpu_custom_call" | custom-call | tf_op jit(solution)/shard_map/pallas_call | solution.py:453
  103.6 1.7 %copy.11 = f32[512,128]{1,0:T(8,128)} copy(f32[512,128]{1,0:T(8,128)} %get-tuple-element.8) | data formatting | bytes 524288
  105.3 1.6 %copy.12 = bf16[1,4,128,128]{3,2,1,0:T(8,128)(2,1)} copy(bf16[1,4,128,128]{3,2,1,0:T(8,128)(2,1)} %bitcast.7) | data formatting | bytes 262144

commit v2 on v1

--- a/solution.py
+++ b/solution.py
@@ -10,6 +10,7 @@
 
 CAP = 2
 ITERS = 2
+PARTS = 2
 MESH = pl.DeviceIdType.MESH
 F32 = jnp.float32
 BF16 = jnp.bfloat16
@@ -69,20 +70,24 @@
     friends = has_up.astype(jnp.int32) + has_dn.astype(jnp.int32) + (nx - 1 + n_space - 1)
     pl.semaphore_wait(barrier, friends)
 
-    def ag_copy(kind, src_a, device):
-        return remote(
-            pix.at[src_a], pix.at[src_a], ag_send.at[kind, src_a], ag_recv.at[src_a], device
-        )
-
-    def ag_copies(src_z, go_up, go_dn):
+    piece = share // PARTS
+
+    def rows_of(h):
+        return pl.ds(h * piece, piece)
+
+    def ag_copy(kind, src_a, h, device):
+        rows = pix.at[src_a, rows_of(h)]
+        return remote(rows, rows, ag_send.at[kind, src_a, h], ag_recv.at[src_a, h], device)
+
+    def ag_copies(src_z, h, go_up, go_dn):
         src_a = src_z * nx + x
         listed = []
         if go_up:
-            listed.append((has_up, ag_copy(0, src_a, at_angle(jnp.minimum(z + 1, nz - 1), x))))
+            listed.append((has_up, ag_copy(0, src_a, h, at_angle(jnp.minimum(z + 1, nz - 1), x))))
         if go_dn:
-            listed.append((has_dn, ag_copy(1, src_a, at_angle(jnp.maximum(z - 1, 0), x))))
+            listed.append((has_dn, ag_copy(1, src_a, h, at_angle(jnp.maximum(z - 1, 0), x))))
         for j, xx in enumerate(x_peers):
-            listed.append((None, ag_copy(2 + j, src_a, at_angle(z, xx))))
+            listed.append((None, ag_copy(2 + j, src_a, h, at_angle(z, xx))))
         return listed
 
     def each(listed, act):
@@ -98,37 +103,40 @@
     def wait_send(copy):
         copy.wait_send()
 
-    def ag_wait(src_a):
-        ag_copy(0, src_a, (me_s, me_a)).wait_recv()
+    def ag_wait(src_a, h):
+        ag_copy(0, src_a, h, (me_s, me_a)).wait_recv()
 
     def gather(work):
-        each(ag_copies(z, True, True), start)
-        work(0)
+        for h in range(PARTS):
+            each(ag_copies(z, h, True, True), start)
+        work(0, PARTS - 1)
         for k in range(1, nz):
-
-            @pl.when(z - k >= 0)
-            def _():
-                ag_wait((z - k) * nx + x)
-                each(ag_copies(z - k, True, False), start)
-
-            @pl.when(z + k < nz)
-            def _():
-                ag_wait((z + k) * nx + x)
-                each(ag_copies(z + k, False, True), start)
-
-            work(k)
+            for h in range(PARTS):
+
+                @pl.when(z - k >= 0)
+                def _():
+                    ag_wait((z - k) * nx + x, h)
+                    each(ag_copies(z - k, h, True, False), start)
+
+                @pl.when(z + k < nz)
+                def _():
+                    ag_wait((z + k) * nx + x, h)
+                    each(ag_copies(z + k, h, False, True), start)
+
+                work(k, h)
 
     def gather_end():
-        each(ag_copies(z, True, True), wait_send)
-        for k in range(1, nz):
-
-            @pl.when(z - k >= 0)
-            def _():
-                each(ag_copies(z - k, True, False), wait_send)
-
-            @pl.when(z + k < nz)
-            def _():
-                each(ag_copies(z + k, False, True), wait_send)
+        for h in range(PARTS):
+            each(ag_copies(z, h, True, True), wait_send)
+            for k in range(1, nz):
+
+                @pl.when(z - k >= 0)
+                def _():
+                    each(ag_copies(z - k, h, True, False), wait_send)
+
+                @pl.when(z + k < nz)
+                def _():
+                    each(ag_copies(z + k, h, False, True), wait_send)
 
     def prepare():
         rays = [ray_list[0, j] for j in range(slots)]
@@ -192,26 +200,44 @@
     def project(c):
         acc[0 : seats * edge] += jnp.dot(mat[c], pix[c], preferred_element_type=F32)
 
-    def first_work(k):
-        half = count // 2
+    def first_work(k, h):
+        slot = max(k - 1, 0) * PARTS + h
+        splits = max((nz - 1) * PARTS, 1)
+        turns = max(splits - PARTS, 1)
         if k == 0:
             prepare()
-            run_tiles(0, half)
-        if k == min(1, nz - 1):
-            run_tiles(half, count)
-        if k == min(2, nz - 1):
+        if k == 0 and nz > 1:
+            return
+        if slot < turns:
+            run_tiles(count * slot // turns, count * (slot + 1) // turns)
+        if slot == splits - 1:
             build(0, n_angle)
 
     def across_x(src_z):
         for xx in x_peers:
-            ag_wait(src_z * nx + xx)
+            for h in range(PARTS):
+                ag_wait(src_z * nx + xx, h)
             project(src_z * nx + xx)
 
-    def later_work(k):
+    def later_work(k, h):
         if k == 0:
             acc[...] = jnp.zeros(acc.shape, F32)
             project(me_a)
             return
+        if h < PARTS - 1:
+            if k == 1:
+                across_x(z)
+                return
+
+            @pl.when(z - k + 1 >= 0)
+            def _():
+                across_x(z - k + 1)
+
+            @pl.when(z + k - 1 < nz)
+            def _():
+                across_x(z + k - 1)
+
+            return
 
         @pl.when(z - k >= 0)
         def _():
@@ -220,18 +246,6 @@
         @pl.when(z + k < nz)
         def _():
             project((z + k) * nx + x)
-
-        if k == 1:
-            across_x(z)
-        else:
-
-            @pl.when(z - k + 1 >= 0)
-            def _():
-                across_x(z - k + 1)
-
-            @pl.when(z + k - 1 < nz)
-            def _():
-                across_x(z + k - 1)
 
     def later_end():
         k = nz - 1
@@ -248,7 +262,8 @@
         acc[...] = jnp.zeros(acc.shape, F32)
         for zz in range(nz):
             for xx in x_peers:
-                ag_wait(zz * nx + xx)
+                for h in range(PARTS):
+                    ag_wait(zz * nx + xx, h)
 
         @pl.loop(0, n_angle)
         def _(c):
@@ -326,91 +341,101 @@
             ray_copy(j, ss).wait_send()
             back_copy(j, ss).wait_send()
 
-    def gx_copy(dst_z, j, xx):
+    def gx_copy(dst_z, j, h, xx):
+        rows = (dst_z, j, rows_of(h))
+        sem = (dst_z, j, h)
         return remote(
-            grad_out.at[dst_z, j], grad_in.at[dst_z, j], gx_send.at[dst_z, j],
-            gx_recv.at[dst_z, j], at_angle(z, xx),
+            grad_out.at[rows], grad_in.at[rows], gx_send.at[sem], gx_recv.at[sem], at_angle(z, xx)
         )
 
-    def dn_copy(dst_z):
+    def dn_copy(dst_z, h):
+        rows = (dst_z, rows_of(h))
         return remote(
-            chain_out.at[dst_z], chain_dn.at[dst_z], dn_send.at[dst_z], dn_recv.at[dst_z],
+            chain_out.at[rows], chain_dn.at[rows], dn_send.at[dst_z, h], dn_recv.at[dst_z, h],
             at_angle(jnp.maximum(z - 1, 0), x),
         )
 
-    def up_copy(dst_z):
+    def up_copy(dst_z, h):
+        rows = (dst_z, rows_of(h))
         return remote(
-            chain_out.at[dst_z], chain_up.at[dst_z], up_send.at[dst_z], up_recv.at[dst_z],
+            chain_out.at[rows], chain_up.at[rows], up_send.at[dst_z, h], up_recv.at[dst_z, h],
             at_angle(jnp.minimum(z + 1, nz - 1), x),
         )
 
-    def back(c):
-        return jnp.dot(mat_t[c], slot_res[...], preferred_element_type=F32)
-
-    def send_terms(dst_z):
+    def back(c, h):
+        return jnp.dot(mat_t[c, rows_of(h)], slot_res[...], preferred_element_type=F32)
+
+    def send_terms(dst_z, h):
         for j, xx in enumerate(x_peers):
-            grad_out[dst_z, j] = back(dst_z * nx + xx).astype(BF16)
-            gx_copy(dst_z, j, xx).start()
-
-    def sum_terms(dst_z):
-        acc[0:share] = back(dst_z * nx + x)
+            grad_out[dst_z, j, rows_of(h)] = back(dst_z * nx + xx, h).astype(BF16)
+            gx_copy(dst_z, j, h, xx).start()
+
+    def sum_terms(dst_z, h):
+        total = back(dst_z * nx + x, h)
         for j in range(nx - 1):
-            gx_copy(dst_z, j, x_peers[j]).wait_recv()
-            acc[0:share] += grad_in[dst_z, j].astype(F32)
-
-    def add_dn(dst_z):
-        dn_copy(dst_z).wait_recv()
-        acc[0:share] += chain_dn[dst_z].astype(F32)
-
-    def add_up(dst_z):
-        up_copy(dst_z).wait_recv()
-        acc[0:share] += chain_up[dst_z].astype(F32)
+            gx_copy(dst_z, j, h, x_peers[j]).wait_recv()
+            total = total + grad_in[dst_z, j, rows_of(h)].astype(F32)
+        acc[0:piece] = total
+
+    def add_dn(dst_z, h):
+        dn_copy(dst_z, h).wait_recv()
+        acc[0:piece] += chain_dn[dst_z, rows_of(h)].astype(F32)
+
+    def add_up(dst_z, h):
+        up_copy(dst_z, h).wait_recv()
+        acc[0:piece] += chain_up[dst_z, rows_of(h)].astype(F32)
 
     def scatter():
         for k in range(nz - 1, 0, -1):
-
-            @pl.when(z - k >= 0)
-            def _():
-                send_terms(z - k)
-
-            @pl.when(z + k < nz)
-            def _():
-                send_terms(z + k)
-
-        send_terms(z)
+            for h in range(PARTS):
+
+                @pl.when(z - k >= 0)
+                def _():
+                    send_terms(z - k, h)
+
+                @pl.when(z + k < nz)
+                def _():
+                    send_terms(z + k, h)
+
+        for h in range(PARTS):
+            send_terms(z, h)
         for k in range(nz - 1, 0, -1):
-
-            @pl.when(z - k >= 0)
-            def _():
-                sum_terms(z - k)
-                pl.when(has_up)(functools.partial(add_dn, z - k))
-                chain_out[z - k] = acc[0:share].astype(BF16)
-                dn_copy(z - k).start()
-
-            @pl.when(z + k < nz)
-            def _():
-                sum_terms(z + k)
-                pl.when(has_dn)(functools.partial(add_up, z + k))
-                chain_out[z + k] = acc[0:share].astype(BF16)
-                up_copy(z + k).start()
-
-        sum_terms(z)
-        pl.when(has_up)(functools.partial(add_dn, z))
-        pl.when(has_dn)(functools.partial(add_up, z))
-        volume[...] = jnp.maximum(volume[...] - step_size * acc[0:share], 0.0)
+            for h in range(PARTS):
+
+                @pl.when(z - k >= 0)
+                def _():
+                    sum_terms(z - k, h)
+                    pl.when(has_up)(functools.partial(add_dn, z - k, h))
+                    chain_out[z - k, rows_of(h)] = acc[0:piece].astype(BF16)
+                    dn_copy(z - k, h).start()
+
+                @pl.when(z + k < nz)
+                def _():
+                    sum_terms(z + k, h)
+                    pl.when(has_dn)(functools.partial(add_up, z + k, h))
+                    chain_out[z + k, rows_of(h)] = acc[0:piece].astype(BF16)
+                    up_copy(z + k, h).start()
+
+        for h in range(PARTS):
+            sum_terms(z, h)
+            pl.when(has_up)(functools.partial(add_dn, z, h))
+            pl.when(has_dn)(functools.partial(add_up, z, h))
+            rows = rows_of(h)
+            volume[rows] = jnp.maximum(volume[rows] - step_size * acc[0:piece], 0.0)
 
     def scatter_end():
         for dst_z in range(nz):
-            for j, xx in enumerate(x_peers):
-                gx_copy(dst_z, j, xx).wait_send()
-
-            @pl.when(z > dst_z)
-            def _():
-                dn_copy(dst_z).wait_send()
-
-            @pl.when(z < dst_z)
-            def _():
-                up_copy(dst_z).wait_send()
+            for h in range(PARTS):
+                for j, xx in enumerate(x_peers):
+                    gx_copy(dst_z, j, h, xx).wait_send()
+
+                @pl.when(z > dst_z)
+                def _():
+                    dn_copy(dst_z, h).wait_send()
+
+                @pl.when(z < dst_z)
+                def _():
+                    up_copy(dst_z, h).wait_send()
 
     for iteration in range(ITERS):
         if iteration == 0:
@@ -426,6 +451,11 @@
         exchange_end()
         scatter_end()
     residual[...] = ray_res[0:own]
+
+
+def hand_out(volume, residual, volume_out, residual_out):
+    volume_out[...] = volume[...]
+    residual_out[...] = residual[...]
 
 
 def shards(image, tiles, tile_slot, tile_block, slot_ray, sinogram, weights):
@@ -486,18 +516,27 @@
             vmem((n_space, 8, 128), jnp.int32),
             pltpu.SMEM((n_space, 8, 128), jnp.int32),
             dma((2,)),
-            dma((2 + sides, n_angle)), dma((n_angle,)),
+            dma((2 + sides, n_angle, PARTS)), dma((n_angle, PARTS)),
             dma((others,)), dma((n_space,)),
             dma((others,)), dma((n_space,)),
             dma((others,)), dma((n_space,)),
-            dma((nz, sides)), dma((nz, sides)),
-            dma((nz,)), dma((nz,)),
-            dma((nz,)), dma((nz,)),
+            dma((nz, sides, PARTS)), dma((nz, sides, PARTS)),
+            dma((nz, PARTS)), dma((nz, PARTS)),
+            dma((nz, PARTS)), dma((nz, PARTS)),
         ],
         compiler_params=pltpu.CompilerParams(
             collective_id=0, has_side_effects=True, vmem_limit_bytes=58 * 1024 * 1024
         ),
     )(image, tile_mats, tile_slot, tile_block, slot_ray, sinogram[0], weights[0])
+    volume, residual = pl.pallas_call(
+        hand_out,
+        out_shape=(
+            jax.ShapeDtypeStruct(volume.shape, F32),
+            jax.ShapeDtypeStruct(residual.shape, BF16),
+        ),
+        in_specs=[whole, whole],
+        out_specs=(whole, whole),
+    )(volume, residual)
     return (volume, residual[None])
 
 

time: 107 us -> 98.6 us (0.921)
  Pallas kernels: 103 us -> 97.8 us
  local copies, waits for them, and re-layouts: 3.24 us -> 0 us
    pallas_call x1, Pallas kernels: 103 us -> 96.1 us  [shards(): pl.pallas_call(functools.partial(kernel, dims), out_shape=(jax.ShapeDtype...]
    unnamed x2 -> x0, local copies, waits for them, and re-layouts: 3.24 us -> none
    pallas_call x0 -> x1, Pallas kernels: none -> 1.74 us  [shards(): pl.pallas_call(hand_out, out_shape=(jax.ShapeDtypeStruct(volume.shape, F3...]
where the time goes in v2:
time: 98.6 us; the launch traced here: 98.5 us
  Pallas kernels  97.8 us (99%)
    pallas_call x1, Pallas kernels, shards(): pl.pallas_call(functools.partial(kernel, dims), out_shape=(jax.ShapeDtype...  96.1 us

profile of v2, /device:TPU:0, one launch (start us, length us, event | category | flops | bytes accessed | tf_op | source)
XLA Modules:
  0.0 98.5 jit_solution(6437545163964179518)
XLA Ops:
  0.6 96.1 %shard_map.86 = (f32[512,128]{1,0:T(8,128)}, bf16[4,128,128]{2,1,0:T(8,128)(2,1)}) custom-call(f32[512,128]{1,0:T(8,128)} %image.1, bf16[96,128,128]{2,1,0:T(8,128)(2,1)} %bitcast.4, s32[1,96]{1,0:T(1,128)} %slot_row.1, s32[1,96]{1,0:T(1,128)} %block_row.1, s32[1,8]{1,0:T(1,128)} %ray_list.1, bf16[4,128,128]{2,1,0:T(8,128)(2,1)} %bitcast.5, ...), custom_call_target="tpu_custom_call" | custom-call | tf_op jit(solution)/shard_map/pallas_call | solution.py:483
  96.7 1.7 %shard_map.87 = (f32[512,128]{1,0:T(8,128)}, bf16[4,128,128]{2,1,0:T(8,128)(2,1)}) custom-call(f32[512,128]{1,0:T(8,128)} %get-tuple-element.6.volume, bf16[4,128,128]{2,1,0:T(8,128)(2,1)} %get-tuple-element.7.residual), custom_call_target="tpu_custom_call" | custom-call | tf_op jit(solution)/shard_map/pallas_call | solution.py:531

commit v3 on v2

--- a/solution.py
+++ b/solution.py
@@ -10,7 +10,7 @@
 
 CAP = 2
 ITERS = 2
-PARTS = 2
+PARTS = 4
 MESH = pl.DeviceIdType.MESH
 F32 = jnp.float32
 BF16 = jnp.bfloat16
@@ -185,7 +185,11 @@
             total = tile_v[t].astype(F32) + run_f[table_s[0, t]]
             run_f[t] = total
             tile_v[t] = total.astype(BF16)
-            run_t[t] = total.T.astype(BF16)
+
+    def turn_tiles(begin, end):
+        @pl.loop(begin, end, unroll=math.gcd(end - begin, 4))
+        def _(t):
+            run_t[t] = tile_v[t].astype(F32).T.astype(BF16)
 
     def build(begin, end):
         @pl.loop(begin, end)
@@ -203,15 +207,27 @@
     def first_work(k, h):
         slot = max(k - 1, 0) * PARTS + h
         splits = max((nz - 1) * PARTS, 1)
-        turns = max(splits - PARTS, 1)
+        third = max(splits // 3, 1)
         if k == 0:
             prepare()
         if k == 0 and nz > 1:
             return
-        if slot < turns:
-            run_tiles(count * slot // turns, count * (slot + 1) // turns)
-        if slot == splits - 1:
-            build(0, n_angle)
+
+        def piece_of(total, first, last):
+            if first <= slot < last:
+                steps = last - first
+                return total * (slot - first) // steps, total * (slot - first + 1) // steps
+            return 0, 0
+
+        jobs = (
+            (run_tiles, count, 0, third),
+            (turn_tiles, count, third, 2 * third),
+            (build, n_angle, 2 * third, splits),
+        )
+        for job, total, first, last in jobs:
+            begin, end = piece_of(total, first, last)
+            if end > begin:
+                job(begin, end)
 
     def across_x(src_z):
         for xx in x_peers:
@@ -225,6 +241,8 @@
             project(me_a)
             return
         if h < PARTS - 1:
+            if h != PARTS // 2 - 1:
+                return
             if k == 1:
                 across_x(z)
                 return

time: 98.6 us -> 94.7 us (0.960)
  Pallas kernels: 97.8 us -> 93.9 us
    pallas_call x1, Pallas kernels: 96.1 us -> 92.1 us  [shards(): pl.pallas_call(functools.partial(kernel, dims), out_shape=(jax.ShapeDtype...]
where the time goes in v3:
time: 94.7 us; the launch traced here: 94.5 us
  Pallas kernels  93.9 us (99%)
    pallas_call x1, Pallas kernels, shards(): pl.pallas_call(functools.partial(kernel, dims), out_shape=(jax.ShapeDtype...  92.1 us

profile of v3, /device:TPU:0, one launch (start us, length us, event | category | flops | bytes accessed | tf_op | source)
XLA Modules:
  0.0 94.5 jit_solution(2498741930112791588)
XLA Ops:
  0.6 92.1 %shard_map.86 = (f32[512,128]{1,0:T(8,128)}, bf16[4,128,128]{2,1,0:T(8,128)(2,1)}) custom-call(f32[512,128]{1,0:T(8,128)} %image.1, bf16[96,128,128]{2,1,0:T(8,128)(2,1)} %bitcast.4, s32[1,96]{1,0:T(1,128)} %slot_row.1, s32[1,96]{1,0:T(1,128)} %block_row.1, s32[1,8]{1,0:T(1,128)} %ray_list.1, bf16[4,128,128]{2,1,0:T(8,128)(2,1)} %bitcast.5, ...), custom_call_target="tpu_custom_call" | custom-call | tf_op jit(solution)/shard_map/pallas_call | solution.py:501
  92.8 1.7 %shard_map.87 = (f32[512,128]{1,0:T(8,128)}, bf16[4,128,128]{2,1,0:T(8,128)(2,1)}) custom-call(f32[512,128]{1,0:T(8,128)} %get-tuple-element.6.volume, bf16[4,128,128]{2,1,0:T(8,128)(2,1)} %get-tuple-element.7.residual), custom_call_target="tpu_custom_call" | custom-call | tf_op jit(solution)/shard_map/pallas_call | solution.py:549

commit v4 on v3

--- a/solution.py
+++ b/solution.py
@@ -380,66 +380,72 @@
             at_angle(jnp.minimum(z + 1, nz - 1), x),
         )
 
-    def back(c, h):
-        return jnp.dot(mat_t[c, rows_of(h)], slot_res[...], preferred_element_type=F32)
-
-    def send_terms(dst_z, h):
+    def back(c):
+        return jnp.dot(mat_t[c], slot_res[...], preferred_element_type=F32)
+
+    def side_rows(side, h):
+        return pl.ds(side * share + h * piece, piece)
+
+    def send_terms(dst_z):
         for j, xx in enumerate(x_peers):
-            grad_out[dst_z, j, rows_of(h)] = back(dst_z * nx + xx, h).astype(BF16)
-            gx_copy(dst_z, j, h, xx).start()
-
-    def sum_terms(dst_z, h):
-        total = back(dst_z * nx + x, h)
+            grad_out[dst_z, j] = back(dst_z * nx + xx).astype(BF16)
+            for h in range(PARTS):
+                gx_copy(dst_z, j, h, xx).start()
+
+    def own_terms(dst_z, side):
+        acc[side * share : (side + 1) * share] = back(dst_z * nx + x)
+
+    def sum_terms(dst_z, side, h):
         for j in range(nx - 1):
             gx_copy(dst_z, j, h, x_peers[j]).wait_recv()
-            total = total + grad_in[dst_z, j, rows_of(h)].astype(F32)
-        acc[0:piece] = total
-
-    def add_dn(dst_z, h):
+            acc[side_rows(side, h)] += grad_in[dst_z, j, rows_of(h)].astype(F32)
+
+    def add_dn(dst_z, side, h):
         dn_copy(dst_z, h).wait_recv()
-        acc[0:piece] += chain_dn[dst_z, rows_of(h)].astype(F32)
-
-    def add_up(dst_z, h):
+        acc[side_rows(side, h)] += chain_dn[dst_z, rows_of(h)].astype(F32)
+
+    def add_up(dst_z, side, h):
         up_copy(dst_z, h).wait_recv()
-        acc[0:piece] += chain_up[dst_z, rows_of(h)].astype(F32)
+        acc[side_rows(side, h)] += chain_up[dst_z, rows_of(h)].astype(F32)
+
+    def send_all(k):
+        if k == 0:
+            send_terms(z)
+            return
+        pl.when(z - k >= 0)(functools.partial(send_terms, z - k))
+        pl.when(z + k < nz)(functools.partial(send_terms, z + k))
+
+    def pass_on(k):
+        pl.when(z - k >= 0)(functools.partial(own_terms, z - k, 0))
+        pl.when(z + k < nz)(functools.partial(own_terms, z + k, 1))
+        for h in range(PARTS):
+
+            @pl.when(z - k >= 0)
+            def _():
+                sum_terms(z - k, 0, h)
+                pl.when(has_up)(functools.partial(add_dn, z - k, 0, h))
+                chain_out[z - k, rows_of(h)] = acc[side_rows(0, h)].astype(BF16)
+                dn_copy(z - k, h).start()
+
+            @pl.when(z + k < nz)
+            def _():
+                sum_terms(z + k, 1, h)
+                pl.when(has_dn)(functools.partial(add_up, z + k, 1, h))
+                chain_out[z + k, rows_of(h)] = acc[side_rows(1, h)].astype(BF16)
+                up_copy(z + k, h).start()
 
     def scatter():
+        send_all(nz - 1)
         for k in range(nz - 1, 0, -1):
-            for h in range(PARTS):
-
-                @pl.when(z - k >= 0)
-                def _():
-                    send_terms(z - k, h)
-
-                @pl.when(z + k < nz)
-                def _():
-                    send_terms(z + k, h)
-
+            send_all(k - 1)
+            pass_on(k)
+        own_terms(z, 0)
         for h in range(PARTS):
-            send_terms(z, h)
-        for k in range(nz - 1, 0, -1):
-            for h in range(PARTS):
-
-                @pl.when(z - k >= 0)
-                def _():
-                    sum_terms(z - k, h)
-                    pl.when(has_up)(functools.partial(add_dn, z - k, h))
-                    chain_out[z - k, rows_of(h)] = acc[0:piece].astype(BF16)
-                    dn_copy(z - k, h).start()
-
-                @pl.when(z + k < nz)
-                def _():
-                    sum_terms(z + k, h)
-                    pl.when(has_dn)(functools.partial(add_up, z + k, h))
-                    chain_out[z + k, rows_of(h)] = acc[0:piece].astype(BF16)
-                    up_copy(z + k, h).start()
-
-        for h in range(PARTS):
-            sum_terms(z, h)
-            pl.when(has_up)(functools.partial(add_dn, z, h))
-            pl.when(has_dn)(functools.partial(add_up, z, h))
+            sum_terms(z, 0, h)
+            pl.when(has_up)(functools.partial(add_dn, z, 0, h))
+            pl.when(has_dn)(functools.partial(add_up, z, 0, h))
             rows = rows_of(h)
-            volume[rows] = jnp.maximum(volume[rows] - step_size * acc[0:piece], 0.0)
+            volume[rows] = jnp.maximum(volume[rows] - step_size * acc[side_rows(0, h)], 0.0)
 
     def scatter_end():
         for dst_z in range(nz):
@@ -516,7 +522,7 @@
             vmem((n_angle, seats * edge, share), BF16),
             vmem((n_angle, share, seats * edge), BF16),
             vmem((n_angle, share, slices), BF16),
-            vmem((max(seats * edge, share), slices), F32),
+            vmem((max(seats * edge, 2 * share), slices), F32),
             vmem((seats, edge, slices), BF16),
             vmem((seats + 1, edge, slices), BF16),
             vmem((own + 1, edge, slices), BF16),

time: 94.7 us -> 94.3 us (level)
  no operation moved by 1% of the time
where the time goes in v4:
time: 94.3 us; the launch traced here: 94.1 us
  Pallas kernels  93.5 us (99%)
    pallas_call x1, Pallas kernels, shards(): pl.pallas_call(functools.partial(kernel, dims), out_shape=(jax.ShapeDtype...  91.7 us

profile of v4, /device:TPU:0, one launch (start us, length us, event | category | flops | bytes accessed | tf_op | source)
XLA Modules:
  0.0 94.1 jit_solution(10342991769499559017)
XLA Ops:
  0.6 91.7 %shard_map.86 = (f32[512,128]{1,0:T(8,128)}, bf16[4,128,128]{2,1,0:T(8,128)(2,1)}) custom-call(f32[512,128]{1,0:T(8,128)} %image.1, bf16[96,128,128]{2,1,0:T(8,128)(2,1)} %bitcast.4, s32[1,96]{1,0:T(1,128)} %slot_row.1, s32[1,96]{1,0:T(1,128)} %block_row.1, s32[1,8]{1,0:T(1,128)} %ray_list.1, bf16[4,128,128]{2,1,0:T(8,128)(2,1)} %bitcast.5, ...), custom_call_target="tpu_custom_call" | custom-call | tf_op jit(solution)/shard_map/pallas_call | solution.py:507
  92.4 1.7 %shard_map.87 = (f32[512,128]{1,0:T(8,128)}, bf16[4,128,128]{2,1,0:T(8,128)(2,1)}) custom-call(f32[512,128]{1,0:T(8,128)} %get-tuple-element.6.volume, bf16[4,128,128]{2,1,0:T(8,128)(2,1)} %get-tuple-element.7.residual), custom_call_target="tpu_custom_call" | custom-call | tf_op jit(solution)/shard_map/pallas_call | solution.py:555

commit v5 on v4

--- a/solution.py
+++ b/solution.py
@@ -106,37 +106,89 @@
     def ag_wait(src_a, h):
         ag_copy(0, src_a, h, (me_s, me_a)).wait_recv()
 
+    even = nx == 2 and nz > 2
+
+    def far(h):
+        return even and h >= PARTS // 2
+
+    def twin_copies(src_z, h, go_up, go_dn):
+        src_a = src_z * nx + x_peers[0]
+        listed = []
+        if go_up:
+            listed.append((has_up, ag_copy(0, src_a, h, at_angle(jnp.minimum(z + 1, nz - 1), x))))
+        if go_dn:
+            listed.append((has_dn, ag_copy(1, src_a, h, at_angle(jnp.maximum(z - 1, 0), x))))
+        return listed
+
+    def relay(src_z, end, h, go_up, go_dn, act, await_first):
+        def plain():
+            if await_first:
+                ag_wait(src_z * nx + x, h)
+            each(ag_copies(src_z, h, go_up, go_dn), act)
+
+        def along():
+            if await_first:
+                ag_wait(src_z * nx + x, h)
+            each(ag_copies(src_z, h, go_up, go_dn)[:-1], act)
+            if await_first:
+                ag_wait(src_z * nx + x_peers[0], h)
+            each(twin_copies(src_z, h, go_up, go_dn), act)
+
+        if far(h):
+            pl.when(jnp.logical_not(end))(plain)
+            pl.when(end)(along)
+        else:
+            plain()
+
+    def own_twin(h, act, await_first):
+        def turn():
+            if await_first:
+                ag_wait(z * nx + x_peers[0], h)
+            each(twin_copies(z, h, True, True), act)
+
+        if far(h):
+            pl.when((z == 0) | (z == nz - 1))(turn)
+
     def gather(work):
         for h in range(PARTS):
             each(ag_copies(z, h, True, True), start)
         work(0, PARTS - 1)
         for k in range(1, nz):
             for h in range(PARTS):
+                if k == 1:
+                    own_twin(h, start, True)
 
                 @pl.when(z - k >= 0)
                 def _():
-                    ag_wait((z - k) * nx + x, h)
-                    each(ag_copies(z - k, h, True, False), start)
+                    relay(z - k, z == k, h, True, False, start, True)
 
                 @pl.when(z + k < nz)
                 def _():
-                    ag_wait((z + k) * nx + x, h)
-                    each(ag_copies(z + k, h, False, True), start)
+                    relay(z + k, z == nz - 1 - k, h, False, True, start, True)
 
                 work(k, h)
 
     def gather_end():
         for h in range(PARTS):
             each(ag_copies(z, h, True, True), wait_send)
+            own_twin(h, wait_send, False)
             for k in range(1, nz):
 
                 @pl.when(z - k >= 0)
                 def _():
-                    each(ag_copies(z - k, h, True, False), wait_send)
+                    relay(z - k, z == k, h, True, False, wait_send, False)
 
                 @pl.when(z + k < nz)
                 def _():
-                    each(ag_copies(z + k, h, False, True), wait_send)
+                    relay(z + k, z == nz - 1 - k, h, False, True, wait_send, False)
+
+    def ag_wait_x(src_z, xx):
+        for h in range(PARTS):
+            if far(h):
+                inner = (src_z != 0) & (src_z != nz - 1)
+                pl.when(inner)(functools.partial(ag_wait, src_z * nx + xx, h))
+            else:
+                ag_wait(src_z * nx + xx, h)
 
     def prepare():
         rays = [ray_list[0, j] for j in range(slots)]
@@ -231,8 +283,7 @@
 
     def across_x(src_z):
         for xx in x_peers:
-            for h in range(PARTS):
-                ag_wait(src_z * nx + xx, h)
+            ag_wait_x(src_z, xx)
             project(src_z * nx + xx)
 
     def later_work(k, h):
@@ -244,8 +295,9 @@
             if h != PARTS // 2 - 1:
                 return
             if k == 1:
+                return
+            if k == 2:
                 across_x(z)
-                return
 
             @pl.when(z - k + 1 >= 0)
             def _():
@@ -267,6 +319,10 @@
 
     def later_end():
         k = nz - 1
+        if k < 2:
+            across_x(z)
+            if k < 1:
+                return
 
         @pl.when(z - k >= 0)
         def _():
@@ -280,8 +336,7 @@
         acc[...] = jnp.zeros(acc.shape, F32)
         for zz in range(nz):
             for xx in x_peers:
-                for h in range(PARTS):
-                    ag_wait(zz * nx + xx, h)
+                ag_wait_x(jnp.int32(zz), xx)
 
         @pl.loop(0, n_angle)
         def _(c):

time: 94.3 us -> 92.6 us (0.982)
  Pallas kernels: 93.5 us -> 91.9 us
    pallas_call x1, Pallas kernels: 91.7 us -> 90.1 us  [shards(): pl.pallas_call(functools.partial(kernel, dims), out_shape=(jax.ShapeDtype...]
where the time goes in v5:
time: 92.6 us; the launch traced here: 92.5 us
  Pallas kernels  91.9 us (99%)
    pallas_call x1, Pallas kernels, shards(): pl.pallas_call(functools.partial(kernel, dims), out_shape=(jax.ShapeDtype...  90.1 us

profile of v5, /device:TPU:0, one launch (start us, length us, event | category | flops | bytes accessed | tf_op | source)
XLA Modules:
  0.0 92.5 jit_solution(12501181195769511259)
XLA Ops:
  0.6 90.1 %shard_map.86 = (f32[512,128]{1,0:T(8,128)}, bf16[4,128,128]{2,1,0:T(8,128)(2,1)}) custom-call(f32[512,128]{1,0:T(8,128)} %image.1, bf16[96,128,128]{2,1,0:T(8,128)(2,1)} %bitcast.4, s32[1,96]{1,0:T(1,128)} %slot_row.1, s32[1,96]{1,0:T(1,128)} %block_row.1, s32[1,8]{1,0:T(1,128)} %ray_list.1, bf16[4,128,128]{2,1,0:T(8,128)(2,1)} %bitcast.5, ...), custom_call_target="tpu_custom_call" | custom-call | tf_op jit(solution)/shard_map/pallas_call | solution.py:562
  90.7 1.7 %shard_map.87 = (f32[512,128]{1,0:T(8,128)}, bf16[4,128,128]{2,1,0:T(8,128)(2,1)}) custom-call(f32[512,128]{1,0:T(8,128)} %get-tuple-element.6.volume, bf16[4,128,128]{2,1,0:T(8,128)(2,1)} %get-tuple-element.7.residual), custom_call_target="tpu_custom_call" | custom-call | tf_op jit(solution)/shard_map/pallas_call | solution.py:610

commit v6 on v5

--- a/solution.py
+++ b/solution.py
@@ -334,13 +334,15 @@
 
     def first_end():
         acc[...] = jnp.zeros(acc.shape, F32)
+
+        @pl.loop(0, nz)
+        def _(zz):
+            project(zz * nx + x)
+
         for zz in range(nz):
             for xx in x_peers:
                 ag_wait_x(jnp.int32(zz), xx)
-
-        @pl.loop(0, n_angle)
-        def _(c):
-            project(c)
+                project(zz * nx + xx)
 
     group = CAP * edge
 

time: 92.6 us -> 93.4 us (level)
  no operation moved by 1% of the time
where the time goes in v6:
time: 93.4 us; the launch traced here: 93.3 us
  Pallas kernels  92.6 us (99%)
    pallas_call x1, Pallas kernels, shards(): pl.pallas_call(functools.partial(kernel, dims), out_shape=(jax.ShapeDtype...  90.9 us

profile of v6, /device:TPU:0, one launch (start us, length us, event | category | flops | bytes accessed | tf_op | source)
XLA Modules:
  0.0 93.3 jit_solution(17285316061628693466)
XLA Ops:
  0.6 90.9 %shard_map.86 = (f32[512,128]{1,0:T(8,128)}, bf16[4,128,128]{2,1,0:T(8,128)(2,1)}) custom-call(f32[512,128]{1,0:T(8,128)} %image.1, bf16[96,128,128]{2,1,0:T(8,128)(2,1)} %bitcast.4, s32[1,96]{1,0:T(1,128)} %slot_row.1, s32[1,96]{1,0:T(1,128)} %block_row.1, s32[1,8]{1,0:T(1,128)} %ray_list.1, bf16[4,128,128]{2,1,0:T(8,128)(2,1)} %bitcast.5, ...), custom_call_target="tpu_custom_call" | custom-call | tf_op jit(solution)/shard_map/pallas_call | solution.py:564
  91.5 1.7 %shard_map.87 = (f32[512,128]{1,0:T(8,128)}, bf16[4,128,128]{2,1,0:T(8,128)(2,1)}) custom-call(f32[512,128]{1,0:T(8,128)} %get-tuple-element.6.volume, bf16[4,128,128]{2,1,0:T(8,128)(2,1)} %get-tuple-element.7.residual), custom_call_target="tpu_custom_call" | custom-call | tf_op jit(solution)/shard_map/pallas_call | solution.py:612
